TPU v7x, 128 devices: a whole 4x4x4 slice. The times are simulated.
128 devices in a mesh: rep: 8 (over z, y_hi), slab: 16 (over y_lo, x, core).
Axes of the slice: x: 4, y: 4 (y_hi: 2, y_lo: 2; y = y_hi * 2 + y_lo), z: 4, core: 2. Of those that a mesh axis runs over, the one named last changes fastest.
Arguments:
- feats: bfloat16 [8, 32, 24576], P('rep', None, 'slab'), may hold values from -6 to 6
- tile_weight: bfloat16 [8, 1536, 64, 512], P('rep', 'slab'), may hold values from -0.25 to 0.25
- tile_atom: int32 [8, 1536], P('rep', 'slab'), may hold values from 0 to 23
- tile_cell: int32 [8, 1536], P('rep', 'slab'), may hold values from 0 to 31
- tile_live: int32 [8, 16], P('rep', 'slab'), may hold values from 24 to 96, as said below
- w_mix: bfloat16 [32, 32], replicated, may hold values from -1 to 1
- conv_w: bfloat16 [27, 32, 32], replicated, may hold values from -0.21875 to 0.21875
- cotangent: bfloat16 [8, 32, 24576], P('rep', None, 'slab'), may hold values from -6 to 6
Outputs:
- potential: bfloat16 [8, 32, 24576], P('rep', None, 'slab')
- grad_feats: bfloat16 [8, 32, 24576], P('rep', None, 'slab')
- grad_conv: float32 [27, 32, 32], replicated
- grad_mix: float32 [32, 32], replicated
Inputs may be any that keep to these rules, and one draw needn't show every extreme that they name: The first tile_live slots of a slab's list are live, the rest are ignored; in every system some slab has all 96 slots live. `tile_atom`: atom block within the tile's own slab. `tile_cell`: cell block within the slab's window of 8 planes that starts 2 planes below the slab.
All inputs are finite; a program needn't handle non-finite values.
Results may differ from a plain program's by a relative error of at most 0.013.
Values may be sent and summed in bfloat16 or wider, within the bound.
A program may use at most 128 MiB of HBM per device.

v0:
```python
import math
import jax
import jax.numpy as jnp
from jax import lax
from jax.sharding import PartitionSpec as P

C = 32
GY = 32
GX = 64
ZD = 4
ZH = 2
A_DEV = 1536
TILE_A = 64
TILE_C = 512
PW = 8
NB = 32
NAB = 24


def from_behind(value, axis, steps):
    count = lax.axis_size(axis)
    pairs = [(source, (source + steps) % count) for source in range(count)]
    return lax.ppermute(value, axis, pairs)


def extended_2(block, sides, width):
    for axis, dim in sides:
        count = lax.axis_size(axis)
        forward = [(i, i + 1) for i in range(count - 1)]
        forward.append((count - 1, 0))
        backward = [(target, source) for source, target in forward]
        low = lax.ppermute(
            lax.slice_in_dim(block, block.shape[dim] - width, None, axis=dim), axis, forward
        )
        high = lax.ppermute(lax.slice_in_dim(block, 0, width, axis=dim), axis, backward)
        block = jnp.concatenate([low, block, high], axis=dim)
    return block


def shifted_stack(field):
    planes = field.shape[1]
    shaped = field.reshape(C, planes, GY, GX)
    pieces = []
    for row_off in (-1, 0, 1):
        for col_off in (-1, 0, 1):
            rolled = jnp.roll(shaped, (-row_off, -col_off), (2, 3))
            pieces.append(rolled.reshape(C, planes, GY * GX))
    return jnp.concatenate(pieces, axis=0)


def conv_valid(field, kernel_set):
    planes = field.shape[1] - 2
    stacked = shifted_stack(field)
    result = jnp.zeros((C, planes, GY * GX), jnp.float32)
    for plane_off in range(3):
        kernel = jnp.transpose(kernel_set[plane_off * 9 : (plane_off + 1) * 9], (1, 0, 2)).reshape(
            C, 9 * C
        )
        result = result + jnp.einsum(
            "ok,kpn->opn",
            kernel,
            stacked[:, plane_off : plane_off + planes],
            preferred_element_type=jnp.float32,
        )
    return result


def weight_grad(upstream, field):
    planes = upstream.shape[1]
    stacked = shifted_stack(field)
    collected = []
    for plane_off in range(3):
        product = jnp.einsum(
            "opn,kpn->ok",
            upstream,
            stacked[:, plane_off : plane_off + planes],
            preferred_element_type=jnp.float32,
        )
        collected.append(jnp.transpose(product.reshape(C, 9, C), (1, 0, 2)))
    return jnp.concatenate(collected, axis=0)


def deposit_tiles(source, weights, atom_ids, first_tile, live_tiles):
    blocks = source.reshape(C, NAB, TILE_A)
    picked = jnp.take(blocks, atom_ids, axis=1)
    product = jnp.einsum("ctk,tkn->tcn", picked, weights, preferred_element_type=jnp.float32)
    alive = first_tile + jnp.arange(weights.shape[0], dtype=jnp.int32) < live_tiles
    return jnp.where(alive[:, None, None], product, 0.0)


def collect_tiles(window_blocks, weights, cell_ids, first_tile, live_tiles):
    picked = jnp.take(window_blocks, cell_ids, axis=1)
    product = jnp.einsum("ctn,tkn->tck", picked, weights, preferred_element_type=jnp.float32)
    alive = first_tile + jnp.arange(weights.shape[0], dtype=jnp.int32) < live_tiles
    return jnp.where(alive[:, None, None], product, 0.0)


def over_tiles(tile_fn, operand, weights, source_ids, target_ids, live_tiles, segments):
    products = tile_fn(operand, weights, source_ids, 0, live_tiles)
    return jax.ops.segment_sum(products, target_ids, num_segments=segments)


def fold_rims(window):
    upper_rim = window[:, ZH + ZD :]
    lower_rim = window[:, :ZH]
    from_below = from_behind(upper_rim.astype(jnp.bfloat16), "slab", 1).astype(upper_rim.dtype)
    from_above = from_behind(lower_rim.astype(jnp.bfloat16), "slab", -1).astype(lower_rim.dtype)
    owned = window[:, ZH : ZH + ZD]
    owned = owned.at[:, :ZH].add(from_below)
    owned = owned.at[:, ZD - ZH :].add(from_above)
    return owned


def with_near(field):
    return extended_2(field, (("slab", 1),), 1)


def with_read(field):
    return extended_2(field, (("slab", 1),), ZH)


def local(feats, tile_weight, tile_atom, tile_cell, tile_live, w_mix, conv_w, cotangent):
    atom_feats = feats[0]
    weights = tile_weight[0]
    atom_ids = tile_atom[0]
    cell_ids = tile_cell[0]
    live_tiles = tile_live[0, 0]
    kernel_flip = jnp.transpose(conv_w[::-1], (0, 2, 1))

    def spread_mesh(source):
        sums = over_tiles(deposit_tiles, source, weights, atom_ids, cell_ids, live_tiles, NB)
        window = jnp.transpose(sums, (1, 0, 2)).reshape(C, PW, GY * GX)
        return fold_rims(window)

    def gather_atoms(extended):
        window_blocks = extended.reshape(C, NB, TILE_C)
        sums = over_tiles(
            collect_tiles, window_blocks, weights, cell_ids, atom_ids, live_tiles, NAB
        )
        return jnp.transpose(sums, (1, 0, 2)).reshape(C, A_DEV)

    mixed = jnp.dot(w_mix, atom_feats, preferred_element_type=jnp.float32).astype(jnp.bfloat16)
    density = spread_mesh(mixed).astype(jnp.bfloat16)
    density_near = with_near(density)
    field_mesh = with_read(conv_valid(density_near, conv_w).astype(jnp.bfloat16))
    potential = gather_atoms(field_mesh).astype(jnp.bfloat16)
    mesh_grad = spread_mesh(cotangent[0]).astype(jnp.bfloat16)
    density_grad = with_read(conv_valid(with_near(mesh_grad), kernel_flip).astype(jnp.bfloat16))
    mixed_grad = gather_atoms(density_grad).astype(jnp.bfloat16)
    feats_grad = jnp.dot(w_mix.T, mixed_grad, preferred_element_type=jnp.float32).astype(
        jnp.bfloat16
    )
    conv_part = weight_grad(mesh_grad, density_near)
    mix_part = lax.dot_general(
        mixed_grad, atom_feats, (((1,), (1,)), ((), ())), preferred_element_type=jnp.float32
    )
    conv_total, mix_total = lax.psum((conv_part, mix_part), ("rep", "slab"))
    groups = lax.axis_size("rep") * lax.axis_size("slab")
    conv_scale = math.sqrt(groups * ZD * GY * GX)
    mix_scale = math.sqrt(groups * A_DEV)
    return (potential[None], feats_grad[None], conv_total / conv_scale, mix_total / mix_scale)


def solution(mesh):
    return jax.shard_map(
        local,
        mesh=mesh,
        in_specs=(
            P("rep", None, "slab"),
            P("rep", "slab", None, None),
            P("rep", "slab"),
            P("rep", "slab"),
            P("rep", "slab"),
            P(),
            P(),
            P("rep", None, "slab"),
        ),
        out_specs=(P("rep", None, "slab"), P("rep", None, "slab"), P(), P()),
        check_vma=False,
    )
```

profile of v0, /device:TPU:1, one launch (start us, length us, event | category | flops | bytes accessed | tf_op | source)
XLA Modules:
  0.0 452.7 jit_solution(4543794386522970593)
XLA Ops:
  11.0 6.5 %broadcast_select_fusion.1 = f32[96,32,512]{2,1,0:T(8,128)} fusion(pred[96]{0:T(512)(128)(4,1)S(1)} %iota_compare_fusion, bf16[1,96,64,512]{3,2,1,0:T(8,128)(2,1)} %param.21, bf16[96,32,64]{2,1,0:T(8,128)(2,1)S(1)} %gather_fusion, pred[96]{0:T(512)(128)(4,1)S(1)} %get-tuple-element.115), kind=kOutput, calls=%fused_computation.47 | convolution fusion | flops 203096064 | bytes 12976320 | tf_op jit(solution)/shard_map/ctk,tkn->tcn/dot_general | solution.py:86
  18.2 12.9 %scatter_fusion = f32[32,32,512]{2,1,0:T(8,128)S(1)} fusion(f32[32,32,512]{2,1,0:T(8,128)S(1)} %broadcast.79.clone, s32[96]{0:T(128)S(1)} %bitcast.209, f32[96,32,512]{2,1,0:T(8,128)} %broadcast_select_fusion.1), kind=kCustom, calls=%fused_computation.4 | custom fusion | flops 1572864 | bytes 18874752 | tf_op jit(solution)/shard_map/scatter-add | solution.py:100
  31.1 2.6 copy.46
  38.1 2.6 collective-permute-start
  41.8 6.5 %broadcast_select_fusion = f32[96,32,512]{2,1,0:T(8,128)} fusion(pred[96]{0:T(512)(128)(4,1)S(1)} %iota_compare_fusion, bf16[1,96,64,512]{3,2,1,0:T(8,128)(2,1)} %param.21, bf16[96,32,64]{2,1,0:T(8,128)(2,1)S(1)} %gather_fusion.2, pred[96]{0:T(512)(128)(4,1)S(1)} %get-tuple-element.115), kind=kOutput, calls=%fused_computation.46 | convolution fusion | flops 203096064 | bytes 12976320 | tf_op jit(solution)/shard_map/ctk,tkn->tcn/dot_general | solution.py:86
  48.6 12.9 %scatter_fusion.2 = f32[32,32,512]{2,1,0:T(8,128)S(1)} fusion(f32[32,32,512]{2,1,0:T(8,128)S(1)} %broadcast.79.clone.1, s32[96]{0:T(128)S(1)} %bitcast.210, f32[96,32,512]{2,1,0:T(8,128)} %broadcast_select_fusion), kind=kCustom, calls=%fused_computation.6 | custom fusion | flops 1572864 | bytes 18874752 | tf_op jit(solution)/shard_map/scatter-add | solution.py:100
  80.1 3.1 collective-permute-start.3
  85.2 4.0 collective-permute-start.9
  97.9 2.6 fusion.44
  100.5 2.6 fusion.43
  112.5 2.8 reshape.271
  115.3 3.9 pad_maximum_fusion.8
  119.2 3.9 reshape.269
  123.1 3.9 pad_maximum_fusion.5
  127.0 3.5 reshape.266
  130.5 3.5 reshape.265
  134.0 3.9 pad_maximum_fusion.4
  138.0 3.5 reshape.264
  143.7 3.4 pad_maximum_fusion.6
  147.1 3.5 reshape.267
  150.7 3.9 pad_maximum_fusion.7
  154.6 3.5 reshape.268
  169.3 3.8 fusion.12
  173.2 3.7 fusion.10
  181.9 2.6 fusion.32
  184.6 2.6 fusion.31
  193.8 2.6 fusion.36
  196.4 2.7 fusion.35
  200.7 4.0 pad_maximum_fusion.15
  204.7 2.8 reshape.285
  207.5 3.5 reshape.284
  211.0 4.0 pad_maximum_fusion.14
  215.0 3.5 reshape.283
  218.5 3.9 pad_maximum_fusion.13
  222.4 3.5 reshape.282
  226.0 3.9 pad_maximum_fusion.12
  229.9 3.5 reshape.281
  233.5 3.9 pad_maximum_fusion.11
  237.4 3.5 reshape.280
  242.9 2.7 pad_maximum_fusion.10
  257.9 3.9 collective-permute-start.11
  266.3 3.8 collective-permute-start.5
  270.1 76.8 %all-reduce.2.cloned.1.call-done = f32[27,32,32]{1,2,0:T(8,128)} async-done(((f32[27,32,32]{1,2,0:T(8,128)}), f32[27,32,32]{1,2,0:T(8,128)}) %all-reduce.2.cloned.1.call-update) | async-done | bytes 110608 | tf_op jit(solution)/shard_map/psum | solution.py:157
  353.6 5.6 %fusion.52 = f32[96,32,64]{2,1,0:T(8,128)S(1)} fusion(bf16[1,96,64,512]{3,2,1,0:T(8,128)(2,1)} %param.21, bf16[96,32,512]{2,1,0:T(8,128)(2,1)} %gather_fusion.3, pred[96]{0:T(512)(128)(4,1)S(1)} %get-tuple-element.114, pred[96]{0:T(512)(128)(4,1)S(1)} %iota_compare_fusion), kind=kOutput, calls=%fused_computation.92 | convolution fusion | flops 203096064 | bytes 10223808 | tf_op jit(solution)/shard_map/ctn,tkn->tck/dot_general | solution.py:93
  359.3 4.5 scatter_fusion.3
  365.0 63.5 %psum.15 = f32[32,32]{1,0:T(8,128)S(1)} all-reduce(f32[32,32]{1,0:T(8,128)S(1)} %fusion.69), channel_id=1, replica_groups=mesh['rep'=8,'slab'=16] {'rep','slab'}, use_global_device_ids=true, to_apply=%region_5.8 | all-reduce | flops 1024 | bytes 8192 | tf_op jit(solution)/shard_map/psum | solution.py:157
  434.7 5.6 %fusion.47 = f32[96,32,64]{2,1,0:T(8,128)S(1)} fusion(bf16[1,96,64,512]{3,2,1,0:T(8,128)(2,1)} %param.21, bf16[96,32,512]{2,1,0:T(8,128)(2,1)} %gather_fusion.1, pred[96]{0:T(512)(128)(4,1)S(1)} %get-tuple-element.114, pred[96]{0:T(512)(128)(4,1)S(1)} %iota_compare_fusion), kind=kOutput, calls=%fused_computation.91 | convolution fusion | flops 203096064 | bytes 10223808 | tf_op jit(solution)/shard_map/ctn,tkn->tck/dot_general | solution.py:93
  440.3 4.5 scatter_fusion.1
  (208 shorter events, 108.1 us)
Async XLA Ops:
  7.2 2.1 copy-start
  7.2 339.8 %all-reduce.2.cloned.1.call-start = ((), (), s32[]{:S(2)}) async-start(), calls=%async_computation | async-start | bytes 884736 | tf_op jit(solution)/shard_map/psum | solution.py:157
  35.9 1.4 copy-start.2
  35.9 5.0 %copy-start.30 = (bf16[1,32,1536]{2,1,0:T(8,128)(2,1)S(1)}, bf16[1,32,1536]{2,1,0:T(8,128)(2,1)}, u32[]{:S(2)}) copy-start(bf16[1,32,1536]{2,1,0:T(8,128)(2,1)} %param.27) | copy-start | bytes 294916
  38.1 39.7 %collective-permute-start = (bf16[32,2,2048]{2,0,1:T(8,128)(2,1)}, bf16[32,2,2048]{2,0,1:T(8,128)(2,1)S(1)}, u32[]{:S(2)}, u32[]{:S(2)}) collective-permute-start(bf16[32,2,2048]{2,0,1:T(8,128)(2,1)} %get-tuple-element.97), channel_id=1, source_target_pairs={{0,1},{1,2},{2,3},{3,4},{4,5},{5,6},{6,7},{7,8},{8,9},{9,10},{10,1... | collective-permute-start | bytes 786440 | tf_op jit(solution)/shard_map/ppermute | solution.py:23
  40.7 38.3 %collective-permute-start.1 = (bf16[32,2,2048]{2,0,1:T(8,128)(2,1)}, bf16[32,2,2048]{2,0,1:T(8,128)(2,1)S(1)}, u32[]{:S(2)}, u32[]{:S(2)}) collective-permute-start(bf16[32,2,2048]{2,0,1:T(8,128)(2,1)} %get-tuple-element.96), channel_id=1, source_target_pairs={{0,15},{1,0},{2,1},{3,2},{4,3},{5,4},{6,5},{7,6},{8,7},{9,8},{10,9... | collective-permute-start | bytes 786440 | tf_op jit(solution)/shard_map/ppermute | solution.py:23
  66.3 4.7 %copy-start.19 = (bf16[27,32,32]{2,1,0:T(8,128)(2,1)S(1)}, bf16[27,32,32]{2,1,0:T(8,128)(2,1)}, u32[]{:S(2)}) copy-start(bf16[27,32,32]{2,1,0:T(8,128)(2,1)} %param.26) | copy-start | bytes 165892
  66.3 4.7 %copy-start.3 = (f32[32,8,2048]{2,1,0:T(8,128)S(1)}, f32[32,8,2048]{2,1,0:T(8,128)}, u32[]{:S(2)}) copy-start(f32[32,8,2048]{2,1,0:T(8,128)} %copy-done.2) | copy-start | bytes 6291460
  68.3 14.9 %collective-permute-start.6 = (bf16[32,2,2048]{2,0,1:T(8,128)(2,1)}, bf16[32,2,2048]{2,0,1:T(8,128)(2,1)}, u32[]{:S(2)}, u32[]{:S(2)}) collective-permute-start(bf16[32,2,2048]{2,0,1:T(8,128)(2,1)} %get-tuple-element.95), channel_id=1, source_target_pairs={{0,1},{1,2},{2,3},{3,4},{4,5},{5,6},{6,7},{7,8},{8,9},{9,10},{10,1... | collective-permute-start | bytes 786440 | tf_op jit(solution)/shard_map/ppermute | solution.py:23
  70.0 14.2 %collective-permute-start.7 = (bf16[32,2,2048]{2,0,1:T(8,128)(2,1)}, bf16[32,2,2048]{2,0,1:T(8,128)(2,1)S(1)}, u32[]{:S(2)}, u32[]{:S(2)}) collective-permute-start(bf16[32,2,2048]{2,0,1:T(8,128)(2,1)} %get-tuple-element.94), channel_id=1, source_target_pairs={{0,15},{1,0},{2,1},{3,2},{4,3},{5,4},{6,5},{7,6},{8,7},{9,8},{10,9... | collective-permute-start | bytes 786440 | tf_op jit(solution)/shard_map/ppermute | solution.py:23
  72.3 1.4 copy-start.6
  73.6 1.3 copy-start.4
  73.6 4.2 slice-start.3
  79.0 4.3 copy-start.5
  79.0 4.3 slice-start.2
  79.2 9.9 %collective-permute-start.2 = (bf16[32,1,2048]{2,0,1:T(8,128)(2,1)S(1)}, bf16[32,1,2048]{2,0,1:T(8,128)(2,1)S(1)}, u32[]{:S(2)}, u32[]{:S(2)}) collective-permute-start(bf16[32,1,2048]{2,0,1:T(8,128)(2,1)S(1)} %get-tuple-element.104), channel_id=1, source_target_pairs={{0,1},{1,2},{2,3},{3,4},{4,5},{5,6},{6,7},{7,8},{8,9},{9,10},{10,1... | collective-permute-start | bytes 393224 | tf_op jit(solution)/shard_map/ppermute | solution.py:32
  80.1 9.0 %collective-permute-start.3 = (bf16[32,1,2048]{2,0,1:T(8,128)(2,1)S(1)}, bf16[32,1,2048]{2,0,1:T(8,128)(2,1)S(1)}, u32[]{:S(2)}, u32[]{:S(2)}) collective-permute-start(bf16[32,1,2048]{2,0,1:T(8,128)(2,1)S(1)} %get-tuple-element.105), channel_id=1, source_target_pairs={{1,0},{2,1},{3,2},{4,3},{5,4},{6,5},{7,6},{8,7},{9,8},{10,9},{11,1... | collective-permute-start | bytes 393224 | tf_op jit(solution)/shard_map/ppermute | solution.py:35
  85.2 93.1 %collective-permute-start.8 = (bf16[32,1,2048]{2,0,1:T(8,128)(2,1)}, bf16[32,1,2048]{2,0,1:T(8,128)(2,1)}, u32[]{:S(2)}, u32[]{:S(2)}) collective-permute-start(bf16[32,1,2048]{2,0,1:T(8,128)(2,1)} %get-tuple-element.100), channel_id=1, source_target_pairs={{0,1},{1,2},{2,3},{3,4},{4,5},{5,6},{6,7},{7,8},{8,9},{9,10},{10,1... | collective-permute-start | bytes 393224 | tf_op jit(solution)/shard_map/ppermute | solution.py:32
  85.2 93.1 %collective-permute-start.9 = (bf16[32,1,2048]{2,0,1:T(8,128)(2,1)}, bf16[32,1,2048]{2,0,1:T(8,128)(2,1)}, u32[]{:S(2)}, u32[]{:S(2)}) collective-permute-start(bf16[32,1,2048]{2,0,1:T(8,128)(2,1)} %get-tuple-element.101), channel_id=1, source_target_pairs={{1,0},{2,1},{3,2},{4,3},{5,4},{6,5},{7,6},{8,7},{9,8},{10,9},{11,1... | collective-permute-start | bytes 393224 | tf_op jit(solution)/shard_map/ppermute | solution.py:35
  141.5 2.2 copy-start.7
  160.3 2.3 copy-start.12
  160.3 3.2 copy-start.16
  162.6 1.9 copy-start.21
  162.6 1.9 copy-start.23
  163.5 1.9 copy-start.15
  164.5 1.9 copy-start.9
  165.5 1.9 copy-start.14
  169.3 7.6 %copy-start.1 = (bf16[288,6,2048]{2,0,1:T(8,128)(2,1)S(1)}, bf16[288,6,2048]{2,0,1:T(8,128)(2,1)}, u32[]{:S(2)}) copy-start(bf16[288,6,2048]{2,0,1:T(8,128)(2,1)} %constant_dynamic-update-slice_fusion) | copy-start | bytes 21233668
  248.1 1.4 copy-start.18
  248.1 1.6 copy-start.17
  249.5 1.2 copy-start.13
  250.7 1.3 copy-start.11
  250.8 1.4 copy-start.10
  251.9 1.2 copy-start.8
  253.1 0.9 copy-start.24
  254.0 1.2 copy-start.27
  255.3 1.3 copy-start.26
  255.3 6.6 %slice-start = ((s8[7077888]{0:T(1024)(128)(4,1)}), s8[4194304]{0:T(1024)(128)(4,1)S(1)}, s32[]{:S(2)}) async-start(s8[7077888]{0:T(1024)(128)(4,1)} %bitcast.196), calls=%async_computation.1 | async-start | bytes 8388608
  256.5 5.3 %slice-start.1 = ((s8[7077888]{0:T(1024)(128)(4,1)}), s8[2883584]{0:T(1024)(128)(4,1)S(1)}, s32[]{:S(2)}) async-start(s8[7077888]{0:T(1024)(128)(4,1)} %bitcast.196), calls=%async_computation.2 | async-start | bytes 5767168
  256.5 5.3 %copy-start.25 = (bf16[32,9,32]{0,2,1:T(8,128)(2,1)S(1)}, bf16[32,9,32]{0,2,1:T(8,128)(2,1)}, u32[]{:S(2)}) copy-start(bf16[32,9,32]{0,2,1:T(8,128)(2,1)} %copy.50) | copy-start | bytes 55300
  257.8 91.1 %collective-permute-start.10 = (bf16[32,2,2048]{2,0,1:T(8,128)(2,1)S(1)}, bf16[32,2,2048]{2,0,1:T(8,128)(2,1)S(1)}, u32[]{:S(2)}, u32[]{:S(2)}) collective-permute-start(bf16[32,2,2048]{2,0,1:T(8,128)(2,1)S(1)} %get-tuple-element.98), channel_id=1, source_target_pairs={{0,1},{1,2},{2,3},{3,4},{4,5},{5,6},{6,7},{7,8},{8,9},{9,10},{10,1... | collective-permute-start | bytes 786440 | tf_op jit(solution)/shard_map/ppermute | solution.py:32
  257.9 91.0 %collective-permute-start.11 = (bf16[32,2,2048]{2,0,1:T(8,128)(2,1)S(1)}, bf16[32,2,2048]{2,0,1:T(8,128)(2,1)S(1)}, u32[]{:S(2)}, u32[]{:S(2)}) collective-permute-start(bf16[32,2,2048]{2,0,1:T(8,128)(2,1)S(1)} %get-tuple-element.99), channel_id=1, source_target_pairs={{1,0},{2,1},{3,2},{4,3},{5,4},{6,5},{7,6},{8,7},{9,8},{10,9},{11,1... | collective-permute-start | bytes 786440 | tf_op jit(solution)/shard_map/ppermute | solution.py:35
  261.9 1.2 copy-start.28
  263.1 1.2 copy-start.29
  266.3 162.9 %collective-permute-start.4 = (bf16[32,2,2048]{2,0,1:T(8,128)(2,1)}, bf16[32,2,2048]{2,0,1:T(8,128)(2,1)}, u32[]{:S(2)}, u32[]{:S(2)}) collective-permute-start(bf16[32,2,2048]{2,0,1:T(8,128)(2,1)} %get-tuple-element.102), channel_id=1, source_target_pairs={{0,1},{1,2},{2,3},{3,4},{4,5},{5,6},{6,7},{7,8},{8,9},{9,10},{10,1... | collective-permute-start | bytes 786440 | tf_op jit(solution)/shard_map/ppermute | solution.py:32
  266.3 162.9 %collective-permute-start.5 = (bf16[32,2,2048]{2,0,1:T(8,128)(2,1)S(1)}, bf16[32,2,2048]{2,0,1:T(8,128)(2,1)}, u32[]{:S(2)}, u32[]{:S(2)}) collective-permute-start(bf16[32,2,2048]{2,0,1:T(8,128)(2,1)S(1)} %get-tuple-element.103), channel_id=1, source_target_pairs={{1,0},{2,1},{3,2},{4,3},{5,4},{6,5},{7,6},{8,7},{9,8},{10,9},{11,1... | collective-permute-start | bytes 786440 | tf_op jit(solution)/shard_map/ppermute | solution.py:35
  353.6 5.6 %copy-start.33 = (s32[1,96]{1,0:T(1,128)S(1)}, s32[1,96]{1,0:T(1,128)}, u32[]{:S(2)}) copy-start(s32[1,96]{1,0:T(1,128)} %param.22) | copy-start | bytes 1156
  359.2 4.9 %copy-start.31 = (bf16[32,32]{1,0:T(8,128)(2,1)S(1)}, bf16[32,32]{1,0:T(8,128)(2,1)}, u32[]{:S(2)}) copy-start(bf16[32,32]{1,0:T(8,128)(2,1)} %param.25) | copy-start | bytes 6148
  (3 other events, 1.9 us)
Sparse Core Ops, SparseCore 0:
  200.8 146.0 all-reduce.1
where the time goes:
time: 460 us; the launch traced here: 453 us
  local copies, waits for them, and re-layouts  118 us (26%)
  other arithmetic  115 us (25%)
  waiting for transfers between devices  76.9 us (17%)
  blocking collectives  63.5 us (14%)
  matrix products  42.3 us (9%)
  starting transfers between devices  21.2 us (5%)
  between operations  15.8 us (3%)
    psum x1, waiting for transfers between devices, local(): conv_total, mix_total = lax.psum((conv_part, mix_part), ('rep', 'slab'))  76.8 us
    concatenate x24, other arithmetic, shifted_stack(): rolled = jnp.roll(shaped, (-row_off, -col_off), (2, 3))  69.1 us
    psum x1, blocking collectives, local(): conv_total, mix_total = lax.psum((conv_part, mix_part), ('rep', 'slab'))  63.5 us
    reshape x16, local copies, waits for them, and re-layouts, shifted_stack(): pieces.append(rolled.reshape(C, planes, GY * GX))  51.4 us
    scatter-add x4, other arithmetic, over_tiles(): return jax.ops.segment_sum(products, target_ids, num_segments=segments)  34.8 us
    unnamed x87, local copies, waits for them, and re-layouts  18.3 us
    ppermute x4, starting transfers between devices, extended_2(): lax.ppermute(lax.slice_in_dim(block, 0, width, axis=dim), axis, backward)  14.8 us
    dot_general x2, matrix products, deposit_tiles(): jnp.einsum('ctk,tkn->tcn', picked, weights, preferred_element_type=jnp.fl...  13 us
  transfers between devices with their start and end apart: 13, of which 1 were waited for; matrix products, arithmetic and copies ran while one was open for 44% of the time, Pallas kernels for 0%

commit v1 on v0

--- a/solution.py
+++ b/solution.py
@@ -154,7 +154,7 @@
     mix_part = lax.dot_general(
         mixed_grad, atom_feats, (((1,), (1,)), ((), ())), preferred_element_type=jnp.float32
     )
-    conv_total, mix_total = lax.psum((conv_part, mix_part), ("rep", "slab"))
+    conv_total, mix_total = jax.lax.psum(jax.lax.psum((conv_part, mix_part), "rep"), "slab")
     groups = lax.axis_size("rep") * lax.axis_size("slab")
     conv_scale = math.sqrt(groups * ZD * GY * GX)
     mix_scale = math.sqrt(groups * A_DEV)

time: 460 us -> 550 us (1.20)
  waiting for transfers between devices: 76.9 us -> 135 us
  blocking collectives: 63.5 us -> 91.4 us
    psum x1 -> x2, waiting for transfers between devices: 76.8 us -> 134 us  [the longest x1 114 us: local(): jax.lax.psum(jax.lax.psum((conv_part, mix_part), 'rep'), 'slab')]
    psum x1 -> x2, blocking collectives: 63.5 us -> 91.4 us  [the longest x1 56.3 us: local(): jax.lax.psum(jax.lax.psum((conv_part, mix_part), 'rep'), 'slab')]
  transfers between devices with their start and end apart: 13 -> 14, of which waited for: 1 -> 2; matrix products, arithmetic and copies ran while one was open for 44% -> 37% of each run, Pallas kernels for 0% -> 0%
where the time goes in v1:
time: 550 us; the launch traced here: 540 us
  waiting for transfers between devices  135 us (25%)
  local copies, waits for them, and re-layouts  119 us (22%)
  other arithmetic  115 us (21%)
  blocking collectives  91.4 us (17%)
  matrix products  42.3 us (8%)
  starting transfers between devices  22.9 us (4%)
  between operations  15.8 us (3%)
    psum x1, waiting for transfers between devices, local(): jax.lax.psum(jax.lax.psum((conv_part, mix_part), 'rep'), 'slab')  114 us
    concatenate x24, other arithmetic, shifted_stack(): rolled = jnp.roll(shaped, (-row_off, -col_off), (2, 3))  69 us
    psum x1, blocking collectives, local(): jax.lax.psum(jax.lax.psum((conv_part, mix_part), 'rep'), 'slab')  56.3 us
    reshape x16, local copies, waits for them, and re-layouts, shifted_stack(): pieces.append(rolled.reshape(C, planes, GY * GX))  51.5 us
    psum x1, blocking collectives, local(): jax.lax.psum((conv_part, mix_part), 'rep')  35.1 us
    scatter-add x4, other arithmetic, over_tiles(): return jax.ops.segment_sum(products, target_ids, num_segments=segments)  34.8 us
    psum x1, waiting for transfers between devices, local(): jax.lax.psum((conv_part, mix_part), 'rep')  20.7 us
    unnamed x87, local copies, waits for them, and re-layouts  18.4 us
  transfers between devices with their start and end apart: 14, of which 2 were waited for; matrix products, arithmetic and copies ran while one was open for 37% of the time, Pallas kernels for 0%

profile of v1, /device:TPU:1, one launch (start us, length us, event | category | flops | bytes accessed | tf_op | source)
XLA Modules:
  0.0 540.1 jit_solution(8881976732160677149)
XLA Ops:
  11.0 6.5 %broadcast_select_fusion.1 = f32[96,32,512]{2,1,0:T(8,128)} fusion(pred[96]{0:T(512)(128)(4,1)S(1)} %iota_compare_fusion, bf16[1,96,64,512]{3,2,1,0:T(8,128)(2,1)} %param.21, bf16[96,32,64]{2,1,0:T(8,128)(2,1)S(1)} %gather_fusion, pred[96]{0:T(512)(128)(4,1)S(1)} %get-tuple-element.115), kind=kOutput, calls=%fused_computation.47 | convolution fusion | flops 203096064 | bytes 12976320 | tf_op jit(solution)/shard_map/ctk,tkn->tcn/dot_general | solution.py:86
  18.2 12.9 %scatter_fusion = f32[32,32,512]{2,1,0:T(8,128)S(1)} fusion(f32[32,32,512]{2,1,0:T(8,128)S(1)} %broadcast.79.clone, s32[96]{0:T(128)S(1)} %bitcast.209, f32[96,32,512]{2,1,0:T(8,128)} %broadcast_select_fusion.1), kind=kCustom, calls=%fused_computation.4 | custom fusion | flops 1572864 | bytes 18874752 | tf_op jit(solution)/shard_map/scatter-add | solution.py:100
  31.2 2.6 copy.46
  38.2 2.6 collective-permute-start
  41.9 6.5 %broadcast_select_fusion = f32[96,32,512]{2,1,0:T(8,128)} fusion(pred[96]{0:T(512)(128)(4,1)S(1)} %iota_compare_fusion, bf16[1,96,64,512]{3,2,1,0:T(8,128)(2,1)} %param.21, bf16[96,32,64]{2,1,0:T(8,128)(2,1)S(1)} %gather_fusion.2, pred[96]{0:T(512)(128)(4,1)S(1)} %get-tuple-element.115), kind=kOutput, calls=%fused_computation.46 | convolution fusion | flops 203096064 | bytes 12976320 | tf_op jit(solution)/shard_map/ctk,tkn->tcn/dot_general | solution.py:86
  48.7 12.9 %scatter_fusion.2 = f32[32,32,512]{2,1,0:T(8,128)S(1)} fusion(f32[32,32,512]{2,1,0:T(8,128)S(1)} %broadcast.79.clone.1, s32[96]{0:T(128)S(1)} %bitcast.210, f32[96,32,512]{2,1,0:T(8,128)} %broadcast_select_fusion), kind=kCustom, calls=%fused_computation.6 | custom fusion | flops 1572864 | bytes 18874752 | tf_op jit(solution)/shard_map/scatter-add | solution.py:100
  80.2 3.1 collective-permute-start.3
  85.3 4.0 collective-permute-start.9
  98.1 2.6 fusion.44
  112.6 2.8 reshape.271
  115.4 3.9 pad_maximum_fusion.8
  119.3 3.9 reshape.269
  123.2 3.9 pad_maximum_fusion.5
  127.1 3.5 reshape.266
  130.7 3.5 reshape.265
  134.2 3.9 pad_maximum_fusion.4
  138.1 3.6 reshape.264
  143.9 3.4 pad_maximum_fusion.6
  147.3 3.6 reshape.267
  150.9 3.9 pad_maximum_fusion.7
  154.8 3.5 reshape.268
  169.5 3.8 fusion.12
  173.4 3.7 fusion.10
  182.2 2.6 fusion.32
  194.0 2.6 fusion.36
  196.6 2.8 fusion.35
  201.0 4.0 pad_maximum_fusion.15
  205.0 2.8 reshape.285
  207.8 3.5 reshape.284
  211.3 3.9 pad_maximum_fusion.14
  215.3 3.5 reshape.283
  218.8 3.9 pad_maximum_fusion.13
  222.7 3.5 reshape.282
  226.3 3.9 pad_maximum_fusion.12
  230.2 3.6 reshape.281
  233.8 3.9 pad_maximum_fusion.11
  237.7 3.5 reshape.280
  243.2 2.7 pad_maximum_fusion.10
  258.2 3.9 collective-permute-start.11
  265.9 20.7 %all-reduce.3.cloned.1.call-done = f32[27,32,32]{1,2,0:T(8,128)} async-done(((f32[27,32,32]{1,2,0:T(8,128)}), f32[27,32,32]{1,2,0:T(8,128)}) %all-reduce.3.cloned.1.call-update) | async-done | bytes 110608 | tf_op jit(solution)/shard_map/psum | solution.py:157
  287.3 5.4 collective-permute-start.4
  292.7 113.8 %all-reduce.5.cloned.1.call-done = f32[27,32,32]{1,2,0:T(8,128)} async-done(((f32[27,32,32]{1,2,0:T(8,128)}), f32[27,32,32]{1,2,0:T(8,128)}) %all-reduce.5.cloned.1.call-update) | async-done | bytes 110608 | tf_op jit(solution)/shard_map/psum | solution.py:157
  413.1 5.6 %fusion.52 = f32[96,32,64]{2,1,0:T(8,128)S(1)} fusion(bf16[1,96,64,512]{3,2,1,0:T(8,128)(2,1)} %param.21, bf16[96,32,512]{2,1,0:T(8,128)(2,1)} %gather_fusion.3, pred[96]{0:T(512)(128)(4,1)S(1)} %get-tuple-element.114, pred[96]{0:T(512)(128)(4,1)S(1)} %iota_compare_fusion), kind=kOutput, calls=%fused_computation.92 | convolution fusion | flops 203096064 | bytes 10223808 | tf_op jit(solution)/shard_map/ctn,tkn->tck/dot_general | solution.py:93
  418.8 4.5 scatter_fusion.3
  424.6 35.1 %psum.30 = f32[32,32]{1,0:T(8,128)S(1)} all-reduce(f32[32,32]{1,0:T(8,128)S(1)} %fusion.69), channel_id=1, replica_groups=mesh['rep'=8,'slab'=16] {'rep'}, use_global_device_ids=true, to_apply=%region_6.9 | all-reduce | flops 1024 | bytes 8192 | tf_op jit(solution)/shard_map/psum | solution.py:157
  459.7 56.3 %psum.31 = f32[32,32]{1,0:T(8,128)S(1)} all-reduce(f32[32,32]{1,0:T(8,128)S(1)} %psum.30), channel_id=1, replica_groups=mesh['rep'=8,'slab'=16] {'slab'}, use_global_device_ids=true, to_apply=%region_7.10 | all-reduce | flops 1024 | bytes 8192 | tf_op jit(solution)/shard_map/psum | solution.py:157
  522.1 5.6 %fusion.47 = f32[96,32,64]{2,1,0:T(8,128)S(1)} fusion(bf16[1,96,64,512]{3,2,1,0:T(8,128)(2,1)} %param.21, bf16[96,32,512]{2,1,0:T(8,128)(2,1)} %gather_fusion.1, pred[96]{0:T(512)(128)(4,1)S(1)} %get-tuple-element.114, pred[96]{0:T(512)(128)(4,1)S(1)} %iota_compare_fusion), kind=kOutput, calls=%fused_computation.91 | convolution fusion | flops 203096064 | bytes 10223808 | tf_op jit(solution)/shard_map/ctn,tkn->tck/dot_general | solution.py:93
  527.7 4.5 scatter_fusion.1
  (212 shorter events, 113.4 us)
Async XLA Ops:
  7.2 2.1 copy-start
  7.2 279.4 %all-reduce.3.cloned.1.call-start = ((), (), s32[]{:S(2)}) async-start(), calls=%async_computation | async-start | bytes 884736 | tf_op jit(solution)/shard_map/psum | solution.py:157
  36.0 1.4 copy-start.2
  36.0 5.0 copy-start.30
  38.2 39.8 %collective-permute-start = (bf16[32,2,2048]{2,0,1:T(8,128)(2,1)}, bf16[32,2,2048]{2,0,1:T(8,128)(2,1)S(1)}, u32[]{:S(2)}, u32[]{:S(2)}) collective-permute-start(bf16[32,2,2048]{2,0,1:T(8,128)(2,1)} %get-tuple-element.97), channel_id=1, source_target_pairs={{0,1},{1,2},{2,3},{3,4},{4,5},{5,6},{6,7},{7,8},{8,9},{9,10},{10,1... | collective-permute-start | bytes 786440 | tf_op jit(solution)/shard_map/ppermute | solution.py:23
  40.8 38.3 %collective-permute-start.1 = (bf16[32,2,2048]{2,0,1:T(8,128)(2,1)}, bf16[32,2,2048]{2,0,1:T(8,128)(2,1)S(1)}, u32[]{:S(2)}, u32[]{:S(2)}) collective-permute-start(bf16[32,2,2048]{2,0,1:T(8,128)(2,1)} %get-tuple-element.96), channel_id=1, source_target_pairs={{0,15},{1,0},{2,1},{3,2},{4,3},{5,4},{6,5},{7,6},{8,7},{9,8},{10,9... | collective-permute-start | bytes 786440 | tf_op jit(solution)/shard_map/ppermute | solution.py:23
  66.4 4.7 copy-start.19
  66.4 4.7 copy-start.3
  68.4 15.0 %collective-permute-start.6 = (bf16[32,2,2048]{2,0,1:T(8,128)(2,1)}, bf16[32,2,2048]{2,0,1:T(8,128)(2,1)}, u32[]{:S(2)}, u32[]{:S(2)}) collective-permute-start(bf16[32,2,2048]{2,0,1:T(8,128)(2,1)} %get-tuple-element.95), channel_id=1, source_target_pairs={{0,1},{1,2},{2,3},{3,4},{4,5},{5,6},{6,7},{7,8},{8,9},{9,10},{10,1... | collective-permute-start | bytes 786440 | tf_op jit(solution)/shard_map/ppermute | solution.py:23
  70.1 14.2 %collective-permute-start.7 = (bf16[32,2,2048]{2,0,1:T(8,128)(2,1)}, bf16[32,2,2048]{2,0,1:T(8,128)(2,1)S(1)}, u32[]{:S(2)}, u32[]{:S(2)}) collective-permute-start(bf16[32,2,2048]{2,0,1:T(8,128)(2,1)} %get-tuple-element.94), channel_id=1, source_target_pairs={{0,15},{1,0},{2,1},{3,2},{4,3},{5,4},{6,5},{7,6},{8,7},{9,8},{10,9... | collective-permute-start | bytes 786440 | tf_op jit(solution)/shard_map/ppermute | solution.py:23
  72.4 1.4 copy-start.6
  73.7 1.4 copy-start.4
  73.7 4.3 slice-start.3
  79.1 4.3 copy-start.5
  79.1 4.3 slice-start.2
  79.3 9.9 %collective-permute-start.2 = (bf16[32,1,2048]{2,0,1:T(8,128)(2,1)S(1)}, bf16[32,1,2048]{2,0,1:T(8,128)(2,1)S(1)}, u32[]{:S(2)}, u32[]{:S(2)}) collective-permute-start(bf16[32,1,2048]{2,0,1:T(8,128)(2,1)S(1)} %get-tuple-element.104), channel_id=1, source_target_pairs={{0,1},{1,2},{2,3},{3,4},{4,5},{5,6},{6,7},{7,8},{8,9},{9,10},{10,1... | collective-permute-start | bytes 393224 | tf_op jit(solution)/shard_map/ppermute | solution.py:32
  80.2 9.1 %collective-permute-start.3 = (bf16[32,1,2048]{2,0,1:T(8,128)(2,1)S(1)}, bf16[32,1,2048]{2,0,1:T(8,128)(2,1)S(1)}, u32[]{:S(2)}, u32[]{:S(2)}) collective-permute-start(bf16[32,1,2048]{2,0,1:T(8,128)(2,1)S(1)} %get-tuple-element.105), channel_id=1, source_target_pairs={{1,0},{2,1},{3,2},{4,3},{5,4},{6,5},{7,6},{8,7},{9,8},{10,9},{11,1... | collective-permute-start | bytes 393224 | tf_op jit(solution)/shard_map/ppermute | solution.py:35
  85.3 93.2 %collective-permute-start.8 = (bf16[32,1,2048]{2,0,1:T(8,128)(2,1)}, bf16[32,1,2048]{2,0,1:T(8,128)(2,1)}, u32[]{:S(2)}, u32[]{:S(2)}) collective-permute-start(bf16[32,1,2048]{2,0,1:T(8,128)(2,1)} %get-tuple-element.100), channel_id=1, source_target_pairs={{0,1},{1,2},{2,3},{3,4},{4,5},{5,6},{6,7},{7,8},{8,9},{9,10},{10,1... | collective-permute-start | bytes 393224 | tf_op jit(solution)/shard_map/ppermute | solution.py:32
  85.3 93.2 %collective-permute-start.9 = (bf16[32,1,2048]{2,0,1:T(8,128)(2,1)}, bf16[32,1,2048]{2,0,1:T(8,128)(2,1)}, u32[]{:S(2)}, u32[]{:S(2)}) collective-permute-start(bf16[32,1,2048]{2,0,1:T(8,128)(2,1)} %get-tuple-element.101), channel_id=1, source_target_pairs={{1,0},{2,1},{3,2},{4,3},{5,4},{6,5},{7,6},{8,7},{9,8},{10,9},{11,1... | collective-permute-start | bytes 393224 | tf_op jit(solution)/shard_map/ppermute | solution.py:35
  141.6 2.2 copy-start.7
  160.5 2.3 copy-start.12
  160.5 3.3 copy-start.16
  162.8 2.0 copy-start.21
  162.8 2.0 copy-start.23
  163.8 1.9 copy-start.15
  164.7 1.9 copy-start.9
  165.7 1.9 copy-start.14
  169.5 7.6 %copy-start.1 = (bf16[288,6,2048]{2,0,1:T(8,128)(2,1)S(1)}, bf16[288,6,2048]{2,0,1:T(8,128)(2,1)}, u32[]{:S(2)}) copy-start(bf16[288,6,2048]{2,0,1:T(8,128)(2,1)} %constant_dynamic-update-slice_fusion) | copy-start | bytes 21233668
  201.0 205.5 %all-reduce.5.cloned.1.call-start = ((), (), s32[]{:S(2)}) async-start(), calls=%async_computation.1 | async-start | bytes 884736 | tf_op jit(solution)/shard_map/psum | solution.py:157
  248.4 1.4 copy-start.18
  248.4 1.6 copy-start.17
  249.8 1.2 copy-start.13
  250.9 1.3 copy-start.11
  251.0 1.4 copy-start.10
  252.2 1.2 copy-start.8
  254.3 1.2 copy-start.27
  255.5 1.3 copy-start.26
  255.5 6.6 %slice-start = ((s8[7077888]{0:T(1024)(128)(4,1)}), s8[4194304]{0:T(1024)(128)(4,1)S(1)}, s32[]{:S(2)}) async-start(s8[7077888]{0:T(1024)(128)(4,1)} %bitcast.196), calls=%async_computation.2 | async-start | bytes 8388608
  256.8 5.3 slice-start.1
  256.8 5.3 copy-start.25
  258.1 150.4 %collective-permute-start.10 = (bf16[32,2,2048]{2,0,1:T(8,128)(2,1)S(1)}, bf16[32,2,2048]{2,0,1:T(8,128)(2,1)S(1)}, u32[]{:S(2)}, u32[]{:S(2)}) collective-permute-start(bf16[32,2,2048]{2,0,1:T(8,128)(2,1)S(1)} %get-tuple-element.98), channel_id=1, source_target_pairs={{0,1},{1,2},{2,3},{3,4},{4,5},{5,6},{6,7},{7,8},{8,9},{9,10},{10,1... | collective-permute-start | bytes 786440 | tf_op jit(solution)/shard_map/ppermute | solution.py:32
  258.2 150.3 %collective-permute-start.11 = (bf16[32,2,2048]{2,0,1:T(8,128)(2,1)S(1)}, bf16[32,2,2048]{2,0,1:T(8,128)(2,1)S(1)}, u32[]{:S(2)}, u32[]{:S(2)}) collective-permute-start(bf16[32,2,2048]{2,0,1:T(8,128)(2,1)S(1)} %get-tuple-element.99), channel_id=1, source_target_pairs={{1,0},{2,1},{3,2},{4,3},{5,4},{6,5},{7,6},{8,7},{9,8},{10,9},{11,1... | collective-permute-start | bytes 786440 | tf_op jit(solution)/shard_map/ppermute | solution.py:35
  262.1 1.2 copy-start.28
  263.4 1.2 copy-start.29
  287.3 229.2 %collective-permute-start.4 = (bf16[32,2,2048]{2,0,1:T(8,128)(2,1)}, bf16[32,2,2048]{2,0,1:T(8,128)(2,1)}, u32[]{:S(2)}, u32[]{:S(2)}) collective-permute-start(bf16[32,2,2048]{2,0,1:T(8,128)(2,1)} %get-tuple-element.102), channel_id=1, source_target_pairs={{0,1},{1,2},{2,3},{3,4},{4,5},{5,6},{6,7},{7,8},{8,9},{9,10},{10,1... | collective-permute-start | bytes 786440 | tf_op jit(solution)/shard_map/ppermute | solution.py:32
  292.7 223.9 %collective-permute-start.5 = (bf16[32,2,2048]{2,0,1:T(8,128)(2,1)S(1)}, bf16[32,2,2048]{2,0,1:T(8,128)(2,1)}, u32[]{:S(2)}, u32[]{:S(2)}) collective-permute-start(bf16[32,2,2048]{2,0,1:T(8,128)(2,1)S(1)} %get-tuple-element.103), channel_id=1, source_target_pairs={{1,0},{2,1},{3,2},{4,3},{5,4},{6,5},{7,6},{8,7},{9,8},{10,9},{11,1... | collective-permute-start | bytes 786440 | tf_op jit(solution)/shard_map/ppermute | solution.py:35
  413.1 5.6 %copy-start.33 = (s32[1,96]{1,0:T(1,128)S(1)}, s32[1,96]{1,0:T(1,128)}, u32[]{:S(2)}) copy-start(s32[1,96]{1,0:T(1,128)} %param.22) | copy-start | bytes 1156
  418.8 4.9 copy-start.31
  (4 other events, 2.8 us)
Sparse Core Ops, SparseCore 0:
  201.1 85.4 all-reduce.2
  289.2 117.2 all-reduce.4
